TPU v7x, 32 devices: a whole 2x2x4 slice. The times are simulated.
32 devices in a mesh: dp: 8 (over y, x, core), expert: 4 (over z).
Axes of the slice: x: 2, y: 2, z: 4, core: 2. Of those that a mesh axis runs over, the one named last changes fastest.
Arguments:
- tokens: bfloat16 [32768, 1152], P(('dp', 'expert')), may hold values from -7 to 7
- norm_gain: float32 [1152], replicated, may hold values from 0.1 to 1.9
- router_weight: bfloat16 [1152, 4], replicated, may hold values from -1 to 1
- up_weight: bfloat16 [4, 1152, 3072], P('expert'), may hold values from -0.1875 to 0.1875
- down_weight: bfloat16 [4, 3072, 1152], P('expert'), may hold values from -0.625 to 0.625
- routes: int32 [32768, 1], P(('dp', 'expert')), may hold values from 0 to 3
- cotangent: bfloat16 [32768, 1152], P(('dp', 'expert')), may hold values from -6 to 6
Outputs:
- mixed: bfloat16 [32768, 1152], P(('dp', 'expert'))
- input_grad: float32 [32768, 1152], P(('dp', 'expert'))
- gain_grad: float32 [1152], replicated
- router_grad: float32 [1152, 4], replicated
- up_grad: float32 [4, 1152, 3072], P('expert', None, 'dp')
- down_grad: float32 [4, 3072, 1152], P('expert', 'dp')
All inputs are finite; a program needn't handle non-finite values.
Results may differ from a plain program's by a relative error of at most 0.0018.
The roundings to bfloat16 on the way count: a program that leaves them out, or rounds other values in their place, can miss the bound.
Values may be sent and summed in bfloat16 or wider, within the bound.
A program may use at most 192 MiB of HBM per device.

v0:
```python
import jax
import jax.numpy as jnp
from jax import lax
from jax.sharding import PartitionSpec as P

ITERS = 8


norm_epsilon = 1e-06
root_half = 0.7071067811865476
inv_root_two_pi = 0.3989422804014327
highest = lax.Precision.HIGHEST


def gelu_value(values):
    return 0.5 * values * (1.0 + lax.erf(values * root_half))


def gelu_slope(values):
    return (
        0.5 * (1.0 + lax.erf(values * root_half))
        + values * jnp.exp(-0.5 * values * values) * inv_root_two_pi
    )


def contract_last(left, right):
    return lax.dot_general(
        left, right, (((1,), (1,)), ((), ())), preferred_element_type=jnp.float32
    )


def contract_first(left, right):
    return lax.dot_general(
        left, right, (((0,), (0,)), ((), ())), preferred_element_type=jnp.float32
    )


def on_device(tokens, norm_gain, router_weight, up_weight, down_weight, routes, cotangent):
    count = tokens.shape[0]
    width = tokens.shape[1]
    experts = lax.axis_size("expert")
    capacity = 3 * count // (2 * experts)
    total = count * lax.axis_size("dp") * experts
    column_target = total / experts
    inputs = tokens.astype(jnp.float32)
    inv_rms = lax.rsqrt(jnp.mean(inputs * inputs, axis=1, keepdims=True) + norm_epsilon)
    unit = inputs * inv_rms
    normed = (unit * norm_gain).astype(jnp.bfloat16)
    logits = jnp.dot(normed, router_weight, preferred_element_type=jnp.float32)
    start_probs = jnp.exp(logits.T)
    probs = start_probs
    row_totals = []
    after_rows = []
    col_scales = []
    after_cols = []
    for step in range(ITERS):
        row_total = jnp.sum(probs, axis=0, keepdims=True)
        probs = probs / row_total
        row_totals.append(row_total)
        after_rows.append(probs)
        col_total = lax.psum(jnp.sum(probs, axis=1, keepdims=True), ("dp", "expert"))
        scale = column_target / col_total
        probs = probs * scale
        col_scales.append(scale)
        after_cols.append(probs)
    route_rows = routes[:, 0]
    labels = jnp.arange(experts, dtype=jnp.int32)
    selected = (labels[:, None] == route_rows[None, :]).astype(jnp.float32)
    gate = jnp.sum(probs * selected, axis=0)
    onehot = selected.T.astype(jnp.int32)
    position = jnp.sum((jnp.cumsum(onehot, axis=0) - 1) * onehot, axis=1)
    targets = jnp.where(position < capacity, route_rows * capacity + position, experts * capacity)
    sent = jnp.zeros((experts * capacity, width), jnp.bfloat16).at[targets].set(normed, mode="drop")
    sent = sent.reshape(experts, capacity, width)
    w_up = up_weight[0]
    w_down = down_weight[0]
    received = lax.all_to_all(sent, "expert", split_axis=0, concat_axis=0, tiled=True)
    rows = received.reshape(-1, width)
    pre_rows = jnp.dot(rows, w_up, preferred_element_type=jnp.float32)
    act_rows = gelu_value(pre_rows).astype(jnp.bfloat16)
    out_rows = jnp.dot(act_rows, w_down, preferred_element_type=jnp.float32).astype(jnp.bfloat16)
    returned_rows = lax.all_to_all(
        out_rows.reshape(received.shape), "expert", split_axis=0, concat_axis=0, tiled=True
    )
    shape_ff = (received.shape[0], received.shape[1], pre_rows.shape[1])
    returned, pre, act, received = (
        returned_rows,
        pre_rows.reshape(shape_ff),
        act_rows.reshape(shape_ff),
        received,
    )
    gathered = jnp.take(
        returned.reshape(experts * capacity, width), targets, axis=0, mode="fill", fill_value=0
    ).astype(jnp.float32)
    mixed = (inputs + gate[:, None] * gathered).astype(jnp.bfloat16)
    grad_out = cotangent.astype(jnp.float32)
    gate_grad_rows = jnp.sum(grad_out * gathered, axis=1)
    back_grad = (
        jnp.zeros((experts * capacity, width), jnp.float32)
        .at[targets]
        .set(gate[:, None] * grad_out, mode="drop")
    )
    back_grad = back_grad.astype(jnp.bfloat16).reshape(experts, capacity, width)
    grad_recv = lax.all_to_all(back_grad, "expert", split_axis=0, concat_axis=0, tiled=True)
    grad_rows = grad_recv.reshape(-1, width)
    pre_rows = pre.reshape(grad_rows.shape[0], -1)
    act_rows = act.reshape(grad_rows.shape[0], -1)
    recv_rows = received.reshape(-1, width)
    pre_grad = (contract_last(grad_rows, w_down) * gelu_slope(pre_rows)).astype(jnp.bfloat16)
    sent_grad = contract_last(pre_grad, w_up).astype(jnp.bfloat16).reshape(experts, capacity, width)
    routed = lax.all_to_all(sent_grad, "expert", split_axis=0, concat_axis=0, tiled=True)
    up_part = contract_first(recv_rows, pre_grad)
    down_part = contract_first(act_rows, grad_rows)
    up_grad, down_grad = (
        lax.psum_scatter(up_part[None], "dp", scatter_dimension=2, tiled=True),
        lax.psum_scatter(down_part[None], "dp", scatter_dimension=1, tiled=True),
    )
    probs_grad = selected * gate_grad_rows[None, :]
    for step in reversed(range(ITERS)):
        column_dot = lax.psum(
            jnp.sum(probs_grad * after_cols[step], axis=1, keepdims=True), ("dp", "expert")
        )
        probs_grad = col_scales[step] * (probs_grad - column_dot / column_target)
        row_dot = jnp.sum(probs_grad * after_rows[step], axis=0, keepdims=True)
        probs_grad = (probs_grad - row_dot) / row_totals[step]
    logits_grad = (probs_grad * start_probs).T
    routed_rows = jnp.take(
        routed.reshape(experts * capacity, width), targets, axis=0, mode="fill", fill_value=0
    ).astype(jnp.float32)
    normed_grad = routed_rows + jnp.dot(
        logits_grad, router_weight.astype(jnp.float32).T, precision=highest
    )
    router_local = lax.dot_general(
        normed.astype(jnp.float32), logits_grad, (((0,), (0,)), ((), ())), precision=highest
    )
    gain_local = jnp.sum(normed_grad * unit, axis=0)
    gain_grad, router_grad = lax.psum((gain_local, router_local), ("dp", "expert"))
    unit_grad = normed_grad * norm_gain
    input_grad = grad_out + inv_rms * (
        unit_grad - unit * jnp.mean(unit_grad * unit, axis=1, keepdims=True)
    )
    return (mixed, input_grad, gain_grad, router_grad, up_grad, down_grad)


def solution(mesh):
    in_specs = (
        P(("dp", "expert"), None),
        P(),
        P(),
        P("expert", None, None),
        P("expert", None, None),
        P(("dp", "expert"), None),
        P(("dp", "expert"), None),
    )
    out_specs = (
        P(("dp", "expert"), None),
        P(("dp", "expert"), None),
        P(),
        P(),
        P("expert", None, "dp"),
        P("expert", "dp", None),
    )
    return jax.shard_map(
        on_device, mesh=mesh, in_specs=in_specs, out_specs=out_specs, check_vma=False
    )
```

profile of v0, /device:TPU:0, one launch (start us, length us, event | category | flops | bytes accessed | tf_op | source)
XLA Modules:
  0.0 1214.4 jit_solution(13042468254821630151)
XLA Ops:
  21.4 85.5 %all_to_all.20 = bf16[4,384,1152]{2,1,0:T(8,128)(2,1)S(1)} all-to-all(bf16[4,384,1152]{2,1,0:T(8,128)(2,1)S(1)} %bitcast.111), channel_id=1, replica_groups=mesh['dp'=8,'expert'=4] {'expert'}, dimensions={0} | all-to-all | bytes 7077888 | tf_op jit(solution)/shard_map/all_to_all | solution.py:77
  106.9 15.9 %multiply_convert_fusion = (bf16[1536,3072]{1,0:T(8,128)(2,1)S(1)}, f32[1536,3072]{1,0:T(8,128)}) fusion(bf16[1536,1152]{1,0:T(8,128)(2,1)S(1)} %bitcast.113, bf16[1,1152,3072]{2,1,0:T(8,128)(2,1)S(1)} %copy-done.37), kind=kOutput, calls=%fused_computation.11 | convolution fusion | flops 10895228928 | bytes 38928384 | tf_op jit(solution)/shard_map/dot_general | solution.py:79
  144.9 94.2 %psum.126 = f32[4,1]{0,1:T(1,128)} all-reduce(f32[4,1]{0,1:T(1,128)} %bitcast.133), channel_id=1, replica_groups=mesh['dp'=8,'expert'=4] {'dp','expert'}, use_global_device_ids=true, to_apply=%region_3.0 | all-reduce | flops 4 | bytes 32 | tf_op jit(solution)/shard_map/psum | solution.py:61
  243.1 38.8 %psum.127 = f32[4,1]{0,1:T(1,128)} all-reduce(f32[4,1]{0,1:T(1,128)} %bitcast.134), channel_id=1, replica_groups=mesh['dp'=8,'expert'=4] {'dp','expert'}, use_global_device_ids=true, to_apply=%region_6.0 | all-reduce | flops 4 | bytes 32 | tf_op jit(solution)/shard_map/psum | solution.py:61
  286.0 41.9 %psum.128 = f32[4,1]{0,1:T(1,128)} all-reduce(f32[4,1]{0,1:T(1,128)} %bitcast.135), channel_id=1, replica_groups=mesh['dp'=8,'expert'=4] {'dp','expert'}, use_global_device_ids=true, to_apply=%region_9.0 | all-reduce | flops 4 | bytes 32 | tf_op jit(solution)/shard_map/psum | solution.py:61
  332.1 38.9 %psum.129 = f32[4,1]{0,1:T(1,128)} all-reduce(f32[4,1]{0,1:T(1,128)} %bitcast.136), channel_id=1, replica_groups=mesh['dp'=8,'expert'=4] {'dp','expert'}, use_global_device_ids=true, to_apply=%region_12.0 | all-reduce | flops 4 | bytes 32 | tf_op jit(solution)/shard_map/psum | solution.py:61
  375.0 41.9 %psum.130 = f32[4,1]{0,1:T(1,128)} all-reduce(f32[4,1]{0,1:T(1,128)} %bitcast.137), channel_id=1, replica_groups=mesh['dp'=8,'expert'=4] {'dp','expert'}, use_global_device_ids=true, to_apply=%region_15.0 | all-reduce | flops 4 | bytes 32 | tf_op jit(solution)/shard_map/psum | solution.py:61
  421.0 38.8 %psum.131 = f32[4,1]{0,1:T(1,128)} all-reduce(f32[4,1]{0,1:T(1,128)} %bitcast.138), channel_id=1, replica_groups=mesh['dp'=8,'expert'=4] {'dp','expert'}, use_global_device_ids=true, to_apply=%region_18.0 | all-reduce | flops 4 | bytes 32 | tf_op jit(solution)/shard_map/psum | solution.py:61
  463.9 42.0 %psum.132 = f32[4,1]{0,1:T(1,128)} all-reduce(f32[4,1]{0,1:T(1,128)} %bitcast.139), channel_id=1, replica_groups=mesh['dp'=8,'expert'=4] {'dp','expert'}, use_global_device_ids=true, to_apply=%region_21.0 | all-reduce | flops 4 | bytes 32 | tf_op jit(solution)/shard_map/psum | solution.py:61
  510.0 38.8 %psum.133 = f32[4,1]{0,1:T(1,128)} all-reduce(f32[4,1]{0,1:T(1,128)} %bitcast.140), channel_id=1, replica_groups=mesh['dp'=8,'expert'=4] {'dp','expert'}, use_global_device_ids=true, to_apply=%region_24.0 | all-reduce | flops 4 | bytes 32 | tf_op jit(solution)/shard_map/psum | solution.py:61
  561.9 41.9 %psum.134 = f32[4,1]{0,1:T(1,128)S(1)} all-reduce(f32[4,1]{0,1:T(1,128)S(1)} %bitcast.142), channel_id=1, replica_groups=mesh['dp'=8,'expert'=4] {'dp','expert'}, use_global_device_ids=true, to_apply=%region_33.35 | all-reduce | flops 4 | bytes 32 | tf_op jit(solution)/shard_map/psum | solution.py:120
  616.9 81.4 %all_to_all.21 = bf16[4,384,1152]{2,1,0:T(8,128)(2,1)S(1)} all-to-all(bf16[4,384,1152]{2,1,0:T(8,128)(2,1)S(1)} %bitcast.112), channel_id=1, replica_groups=mesh['dp'=8,'expert'=4] {'expert'}, dimensions={0} | all-to-all | bytes 7077888 | tf_op jit(solution)/shard_map/all_to_all | solution.py:104
  698.3 20.7 %fusion.5 = bf16[1536,3072]{1,0:T(8,128)(2,1)S(1)} fusion(f32[1536,3072]{1,0:T(8,128)} %get-tuple-element.46, bf16[1536,1152]{1,0:T(8,128)(2,1)S(1)} %bitcast.117, bf16[1,3072,1152]{2,1,0:T(8,128)(2,1)} %param.13), kind=kOutput, calls=%fused_computation.10 | convolution fusion | flops 10918821888 | bytes 38928384 | tf_op jit(solution)/shard_map/dot_general | solution.py:27
  722.6 14.1 %convolution_bitcast_fusion = f32[1,1152,3072]{2,1,0:T(8,128)} fusion(bf16[1536,1152]{1,0:T(8,128)(2,1)S(1)} %bitcast.114, bf16[1536,3072]{1,0:T(8,128)(2,1)S(1)} %fusion.5), kind=kOutput, calls=%fused_computation.13 | convolution fusion | flops 10871635968 | bytes 27131904 | tf_op jit(solution)/shard_map/dot_general | solution.py:33
  737.0 17.9 %convolution_bitcast_fusion.1 = f32[1,3072,1152]{2,1,0:T(8,128)} fusion(bf16[1536,3072]{1,0:T(8,128)(2,1)} %copy-done.39, bf16[1536,1152]{1,0:T(8,128)(2,1)S(1)} %bitcast.118), kind=kOutput, calls=%fused_computation.14 | convolution fusion | flops 10871635968 | bytes 27131904 | tf_op jit(solution)/shard_map/dot_general | solution.py:33
  755.0 18.3 %convolution_convert_fusion = bf16[1536,1152]{1,0:T(8,128)(2,1)} fusion(bf16[1536,3072]{1,0:T(8,128)(2,1)} %copy-done.38, bf16[1,1152,3072]{2,1,0:T(8,128)(2,1)} %param.12), kind=kOutput, calls=%fused_computation.15 | convolution fusion | flops 10873405440 | bytes 20054016 | tf_op jit(solution)/shard_map/dot_general | solution.py:27
  778.6 97.4 %psum.135 = f32[4,1]{0,1:T(1,128)} all-reduce(f32[4,1]{0,1:T(1,128)} %bitcast.141), channel_id=1, replica_groups=mesh['dp'=8,'expert'=4] {'dp','expert'}, use_global_device_ids=true, to_apply=%region_36.38 | all-reduce | flops 4 | bytes 32 | tf_op jit(solution)/shard_map/psum | solution.py:120
  879.5 39.1 %psum.136 = f32[4,1]{0,1:T(1,128)} all-reduce(f32[4,1]{0,1:T(1,128)} %bitcast.132), channel_id=1, replica_groups=mesh['dp'=8,'expert'=4] {'dp','expert'}, use_global_device_ids=true, to_apply=%region_39.41 | all-reduce | flops 4 | bytes 32 | tf_op jit(solution)/shard_map/psum | solution.py:120
  922.2 42.2 %psum.137 = f32[4,1]{0,1:T(1,128)} all-reduce(f32[4,1]{0,1:T(1,128)} %bitcast.143), channel_id=1, replica_groups=mesh['dp'=8,'expert'=4] {'dp','expert'}, use_global_device_ids=true, to_apply=%region_42.44 | all-reduce | flops 4 | bytes 32 | tf_op jit(solution)/shard_map/psum | solution.py:120
  967.9 38.9 %psum.138 = f32[4,1]{0,1:T(1,128)} all-reduce(f32[4,1]{0,1:T(1,128)} %bitcast.144), channel_id=1, replica_groups=mesh['dp'=8,'expert'=4] {'dp','expert'}, use_global_device_ids=true, to_apply=%region_45.47 | all-reduce | flops 4 | bytes 32 | tf_op jit(solution)/shard_map/psum | solution.py:120
  1010.4 41.8 %psum.139 = f32[4,1]{0,1:T(1,128)} all-reduce(f32[4,1]{0,1:T(1,128)} %bitcast.145), channel_id=1, replica_groups=mesh['dp'=8,'expert'=4] {'dp','expert'}, use_global_device_ids=true, to_apply=%region_48.50 | all-reduce | flops 4 | bytes 32 | tf_op jit(solution)/shard_map/psum | solution.py:120
  1055.9 39.3 %psum.140 = f32[4,1]{0,1:T(1,128)} all-reduce(f32[4,1]{0,1:T(1,128)} %bitcast.146), channel_id=1, replica_groups=mesh['dp'=8,'expert'=4] {'dp','expert'}, use_global_device_ids=true, to_apply=%region_51.53 | all-reduce | flops 4 | bytes 32 | tf_op jit(solution)/shard_map/psum | solution.py:120
  1098.8 41.9 %psum.141 = f32[4,1]{0,1:T(1,128)} all-reduce(f32[4,1]{0,1:T(1,128)} %bitcast.147), channel_id=1, replica_groups=mesh['dp'=8,'expert'=4] {'dp','expert'}, use_global_device_ids=true, to_apply=%region_54.56 | all-reduce | flops 4 | bytes 32 | tf_op jit(solution)/shard_map/psum | solution.py:120
  1160.9 39.5 %all-reduce = (f32[1152]{0:T(1024)}, f32[1152,4]{0,1:T(4,128)}) all-reduce(f32[1152]{0:T(1024)S(1)} %get-tuple-element.7, f32[1152,4]{0,1:T(4,128)S(1)} %copy-done.22), channel_id=1, replica_groups=mesh['dp'=8,'expert'=4] {'dp','expert'}, use_global_device_ids=true, to_apply=%region_58.60 | all-reduce | flops 5760 | bytes 46080 | tf_op jit(solution)/shard_map/psum | solution.py:137
  (165 shorter events, 148.1 us)
Async XLA Ops:
  7.2 133.4 %copy-start = (bf16[1152,4]{0,1:T(4,128)(2,1)S(1)}, bf16[1152,4]{0,1:T(4,128)(2,1)}, u32[]{:S(2)}) copy-start(bf16[1152,4]{0,1:T(4,128)(2,1)} %param.11) | copy-start | bytes 27652
  9.4 97.5 %copy-start.19 = (f32[1024]{0:T(1024)}, f32[1024]{0:T(1024)S(1)}, u32[]{:S(2)}) copy-start(f32[1024]{0:T(1024)S(1)} %add_rsqrt_fusion) | copy-start | bytes 12292
  21.4 85.5 %copy-start.37 = (bf16[1,1152,3072]{2,1,0:T(8,128)(2,1)S(1)}, bf16[1,1152,3072]{2,1,0:T(8,128)(2,1)}, u32[]{:S(2)}) copy-start(bf16[1,1152,3072]{2,1,0:T(8,128)(2,1)} %param.12) | copy-start | bytes 21233668
  21.4 101.5 %slice-start = ((s8[7077888]{0:T(1024)(128)(4,1)}), s8[4194304]{0:T(1024)(128)(4,1)S(1)}, s32[]{:S(2)}) async-start(s8[7077888]{0:T(1024)(128)(4,1)} %bitcast.148), calls=%async_computation.8 | async-start | bytes 8388608
  106.9 16.0 %copy-start.3 = (bf16[4,384,1152]{2,1,0:T(8,128)(2,1)}, bf16[4,384,1152]{2,1,0:T(8,128)(2,1)S(1)}, u32[]{:S(2)}) copy-start(bf16[4,384,1152]{2,1,0:T(8,128)(2,1)S(1)} %all_to_all.20) | copy-start | bytes 10616836
  106.9 16.0 %slice-start.1 = ((s8[7077888]{0:T(1024)(128)(4,1)}), s8[2883584]{0:T(1024)(128)(4,1)S(1)}, s32[]{:S(2)}) async-start(s8[7077888]{0:T(1024)(128)(4,1)} %bitcast.148), calls=%async_computation.9 | async-start | bytes 5767168
  122.9 13.8 %copy-start.39 = (bf16[1536,3072]{1,0:T(8,128)(2,1)}, bf16[1536,3072]{1,0:T(8,128)(2,1)S(1)}, u32[]{:S(2)}) copy-start(bf16[1536,3072]{1,0:T(8,128)(2,1)S(1)} %get-tuple-element.45) | copy-start | bytes 28311556
  136.6 413.4 %copy-start.5 = (s32[1024,1]{0,1:T(1,128)S(1)}, s32[1024,1]{0,1:T(1,128)}, u32[]{:S(2)}) copy-start(s32[1024,1]{0,1:T(1,128)} %param.14) | copy-start | bytes 12292
  136.6 415.9 %all-to-all-start.1 = ((bf16[4,384,1152]{2,1,0:T(8,128)(2,1)}), bf16[4,384,1152]{2,1,0:T(8,128)(2,1)S(1)}, u32[]{:S(2)}, u32[]{:S(2)}) async-start(bf16[4,384,1152]{2,1,0:T(8,128)(2,1)} %bitcast.116), calls=%async_computation.1 | async-start | bytes 7077888 | tf_op jit(solution)/shard_map/all_to_all | solution.py:82
  140.5 1066.6 %reduce-scatter.3.cloned.1.call-start = ((), (), s32[]{:S(2)}) async-start(), calls=%async_computation.6 | async-start | bytes 15925248 | tf_op jit(solution)/shard_map/reduce_scatter | solution.py:115
  558.2 46.3 %copy-start.2 = (bf16[1024,1152]{1,0:T(8,128)(2,1)S(1)}, bf16[1024,1152]{1,0:T(8,128)(2,1)}, u32[]{:S(2)}) copy-start(bf16[1024,1152]{1,0:T(8,128)(2,1)} %param.15) | copy-start | bytes 7077892
  561.7 51.8 %copy-start.7 = (f32[1024]{0:T(1024)}, f32[1024]{0:T(1024)S(1)}, u32[]{:S(2)}) copy-start(f32[1024]{0:T(1024)S(1)} %fusion.23) | copy-start | bytes 12292
  603.8 9.7 copy-start.32
  604.5 9.1 copy-start.10
  698.3 24.3 %copy-start.4 = (bf16[4,384,1152]{2,1,0:T(8,128)(2,1)S(1)}, bf16[4,384,1152]{2,1,0:T(8,128)(2,1)}, u32[]{:S(2)}) copy-start(bf16[4,384,1152]{2,1,0:T(8,128)(2,1)} %copy-done.3) | copy-start | bytes 10616836
  736.8 470.3 %reduce-scatter.5.cloned.1.call-start = ((), (), s32[]{:S(2)}) async-start(), calls=%async_computation.7 | async-start | bytes 15925248 | tf_op jit(solution)/shard_map/reduce_scatter | solution.py:116
  773.3 373.1 %all-to-all-start.3 = ((bf16[4,384,1152]{2,1,0:T(8,128)(2,1)}), bf16[4,384,1152]{2,1,0:T(8,128)(2,1)S(1)}, u32[]{:S(2)}, u32[]{:S(2)}) async-start(bf16[4,384,1152]{2,1,0:T(8,128)(2,1)} %bitcast.115), calls=%async_computation.3 | async-start | bytes 7077888 | tf_op jit(solution)/shard_map/all_to_all | solution.py:111
  879.5 266.9 %copy-start.12 = (s32[1024]{0:T(1024)S(1)}, s32[1024]{0:T(1024)}, u32[]{:S(2)}) copy-start(s32[1024]{0:T(1024)} %broadcast_clamp_fusion) | copy-start | bytes 12292
  1151.9 9.0 copy-start.22
  1151.9 48.4 %copy-start.1 = (bf16[1024,1152]{1,0:T(8,128)(2,1)S(1)}, bf16[1024,1152]{1,0:T(8,128)(2,1)}, u32[]{:S(2)}) copy-start(bf16[1024,1152]{1,0:T(8,128)(2,1)} %param.9) | copy-start | bytes 7077892
  1151.9 48.4 %copy-start.11 = (f32[1024]{0:T(1024)S(1)}, f32[1024]{0:T(1024)}, u32[]{:S(2)}) copy-start(f32[1024]{0:T(1024)} %copy-done.10) | copy-start | bytes 12292
  1151.9 48.4 %copy-start.20 = (f32[1024]{0:T(1024)S(1)}, f32[1024]{0:T(1024)}, u32[]{:S(2)}) copy-start(f32[1024]{0:T(1024)} %copy-done.19) | copy-start | bytes 12292
  1151.9 48.4 %copy-start.21 = (f32[1152]{0:T(1024)S(1)}, f32[1152]{0:T(1024)}, u32[]{:S(2)}) copy-start(f32[1152]{0:T(1024)} %param.10) | copy-start | bytes 13828
  1151.9 48.4 %copy-start.31 = (pred[1024]{0:T(1024)(128)(4,1)S(1)}, pred[1024]{0:T(1024)(128)(4,1)}, u32[]{:S(2)}) copy-start(pred[1024]{0:T(1024)(128)(4,1)} %compare_and_fusion) | copy-start | bytes 3076
  (22 other events, 43.9 us)
Sparse Core Ops, SparseCore 0:
  736.9 100.3 reduce-scatter.2
  841.5 102.5 reduce-scatter.4
where the time goes:
time: 1230 us; the launch traced here: 1210 us
  blocking collectives  964 us (78%)
  matrix products  116 us (9%)
  other arithmetic  90.9 us (7%)
  local copies, waits for them, and re-layouts  20.4 us (2%)
  between operations  14.9 us (1%)
    psum x8, blocking collectives, on_device(): lax.psum(jnp.sum(probs_grad * after_cols[step], axis=1, keepdims=True), (...  383 us
    psum x8, blocking collectives, on_device(): lax.psum(jnp.sum(probs, axis=1, keepdims=True), ('dp', 'expert'))  375 us
    all_to_all x1, blocking collectives, on_device(): lax.all_to_all(sent, 'expert', split_axis=0, concat_axis=0, tiled=True)  85.5 us
    all_to_all x1, blocking collectives, on_device(): lax.all_to_all(back_grad, 'expert', split_axis=0, concat_axis=0, tiled=True)  81.4 us
    psum x1, blocking collectives, on_device(): lax.psum((gain_local, router_local), ('dp', 'expert'))  39.5 us
    dot_general x2, matrix products, contract_last(): lax.dot_general(left, right, (((1,), (1,)), ((), ())), preferred_element_...  39 us
    dot_general x2, matrix products, contract_first(): lax.dot_general(left, right, (((0,), (0,)), ((), ())), preferred_element_...  32 us
  transfers between devices with their start and end apart: 4, of which 0 were waited for; matrix products, arithmetic and copies ran while one was open for 10% of the time, Pallas kernels for 0%

commit v1 on v0

--- a/solution.py
+++ b/solution.py
@@ -1,6 +1,10 @@
+import functools
+
 import jax
 import jax.numpy as jnp
 from jax import lax
+from jax.experimental import pallas as pl
+from jax.experimental.pallas import tpu as pltpu
 from jax.sharding import PartitionSpec as P
 
 ITERS = 8
@@ -21,6 +25,93 @@
         0.5 * (1.0 + lax.erf(values * root_half))
         + values * jnp.exp(-0.5 * values * values) * inv_root_two_pi
     )
+
+
+def total_of(values):
+    return jnp.sum(jnp.sum(values, axis=0, keepdims=True), axis=1, keepdims=True)
+
+
+def balance_forward(target, logits_ref, probs_ref, rows_ref, scales_ref):
+    blocks, experts = logits_ref.shape[:2]
+
+    def step_pass(step, scales):
+        def block(n, sums):
+            if scales is None:
+                held = [jnp.exp(logits_ref[n, e]) for e in range(experts)]
+            else:
+                held = [probs_ref[n, e] * scales[e] for e in range(experts)]
+            row_total = sum(held[1:], held[0])
+            rows_ref[step, n] = row_total
+            after = [h / row_total for h in held]
+            for e in range(experts):
+                probs_ref[n, e] = after[e]
+            return tuple(s + a for s, a in zip(sums, after))
+
+        zero = tuple(jnp.zeros(logits_ref.shape[2:], jnp.float32) for _ in range(experts))
+        sums = lax.fori_loop(0, blocks, block, zero)
+        made = [target / total_of(s) for s in sums]
+        for e in range(experts):
+            scales_ref[step, e] = jnp.broadcast_to(made[e], logits_ref.shape[2:])
+        return made
+
+    scales = None
+    for step in range(ITERS):
+        scales = step_pass(step, scales)
+
+    def last(n, carry):
+        for e in range(experts):
+            probs_ref[n, e] = probs_ref[n, e] * scales[e]
+        return carry
+
+    lax.fori_loop(0, blocks, last, 0)
+
+
+def balance_backward(target, probs_ref, rows_ref, scales_ref, grads_ref, out_ref, held_ref):
+    blocks, experts = probs_ref.shape[:2]
+    zero = tuple(jnp.zeros(probs_ref.shape[2:], jnp.float32) for _ in range(experts))
+
+    def first(n, dots):
+        made = []
+        for e in range(experts):
+            held = probs_ref[n, e]
+            grad = grads_ref[n, e]
+            held_ref[n, e] = held
+            out_ref[n, e] = grad
+            made.append(dots[e] + held * grad)
+        return tuple(made)
+
+    dots = lax.fori_loop(0, blocks, first, zero)
+    for step in reversed(range(ITERS)):
+        means = [total_of(d) / target for d in dots]
+        scales = [scales_ref[step, e] for e in range(experts)]
+        inverse = [1.0 / s for s in scales]
+
+        def block(n, dots):
+            row_total = rows_ref[step, n]
+            grads = [scales[e] * (out_ref[n, e] - means[e]) for e in range(experts)]
+            held = [held_ref[n, e] * inverse[e] for e in range(experts)]
+            row_dot = sum((g * h for g, h in zip(grads, held)))
+            made = []
+            for e in range(experts):
+                grad = (grads[e] - row_dot) / row_total
+                before = held[e] * row_total
+                out_ref[n, e] = grad
+                held_ref[n, e] = before
+                made.append(dots[e] + grad * before)
+            return tuple(made)
+
+        dots = lax.fori_loop(0, blocks, block, zero)
+
+
+def in_vmem(kernel, outs, scratch, *arrays):
+    return pl.pallas_call(
+        kernel,
+        out_shape=outs,
+        in_specs=[pl.BlockSpec(memory_space=pltpu.VMEM)] * len(arrays),
+        out_specs=jax.tree.map(lambda _: pl.BlockSpec(memory_space=pltpu.VMEM), outs),
+        scratch_shapes=scratch,
+        compiler_params=pltpu.CompilerParams(vmem_limit_bytes=60 * 1024 * 1024),
+    )(*arrays)
 
 
 def contract_last(left, right):
@@ -47,22 +138,24 @@
     unit = inputs * inv_rms
     normed = (unit * norm_gain).astype(jnp.bfloat16)
     logits = jnp.dot(normed, router_weight, preferred_element_type=jnp.float32)
+    axes = ("dp", "expert")
+    tile = (experts, 8, count // 8)
     start_probs = jnp.exp(logits.T)
-    probs = start_probs
-    row_totals = []
-    after_rows = []
-    col_scales = []
-    after_cols = []
-    for step in range(ITERS):
-        row_total = jnp.sum(probs, axis=0, keepdims=True)
-        probs = probs / row_total
-        row_totals.append(row_total)
-        after_rows.append(probs)
-        col_total = lax.psum(jnp.sum(probs, axis=1, keepdims=True), ("dp", "expert"))
-        scale = column_target / col_total
-        probs = probs * scale
-        col_scales.append(scale)
-        after_cols.append(probs)
+    all_logits = lax.all_gather(logits.T.reshape(tile), axes)
+    devices = all_logits.shape[0]
+    f32 = jnp.float32
+    all_probs, all_rows, all_scales = in_vmem(
+        functools.partial(balance_forward, column_target),
+        (
+            jax.ShapeDtypeStruct(all_logits.shape, f32),
+            jax.ShapeDtypeStruct((ITERS, devices) + tile[1:], f32),
+            jax.ShapeDtypeStruct((ITERS,) + tile, f32),
+        ),
+        [],
+        all_logits,
+    )
+    me = lax.axis_index(axes)
+    probs = lax.dynamic_index_in_dim(all_probs, me, 0, keepdims=False).reshape(experts, count)
     route_rows = routes[:, 0]
     labels = jnp.arange(experts, dtype=jnp.int32)
     selected = (labels[:, None] == route_rows[None, :]).astype(jnp.float32)
@@ -116,13 +209,17 @@
         lax.psum_scatter(down_part[None], "dp", scatter_dimension=1, tiled=True),
     )
     probs_grad = selected * gate_grad_rows[None, :]
-    for step in reversed(range(ITERS)):
-        column_dot = lax.psum(
-            jnp.sum(probs_grad * after_cols[step], axis=1, keepdims=True), ("dp", "expert")
-        )
-        probs_grad = col_scales[step] * (probs_grad - column_dot / column_target)
-        row_dot = jnp.sum(probs_grad * after_rows[step], axis=0, keepdims=True)
-        probs_grad = (probs_grad - row_dot) / row_totals[step]
+    all_grads = lax.all_gather(probs_grad.reshape(tile), axes)
+    all_grads = in_vmem(
+        functools.partial(balance_backward, column_target),
+        jax.ShapeDtypeStruct(all_logits.shape, f32),
+        [pltpu.VMEM(all_logits.shape, f32)],
+        all_probs,
+        all_rows,
+        all_scales,
+        all_grads,
+    )
+    probs_grad = lax.dynamic_index_in_dim(all_grads, me, 0, keepdims=False).reshape(experts, count)
     logits_grad = (probs_grad * start_probs).T
     routed_rows = jnp.take(
         routed.reshape(experts * capacity, width), targets, axis=0, mode="fill", fill_value=0

time: 1230 us -> 683 us (0.56)
  blocking collectives: 964 us -> 258 us
  waiting for transfers between devices: 0.04 us -> 186 us
  other arithmetic: 90.9 us -> 42.3 us
  Pallas kernels: 0 us -> 13.8 us
    psum x16 -> x0, blocking collectives: 758 us -> none  [the longest x8 383 us: on_device(): lax.psum(jnp.sum(probs_grad * after_cols[step], axis=1, keepdims=True), (...]
    all_gather x0 -> x2, blocking collectives: none -> 219 us  [the longest x1 145 us: on_device(): all_logits = lax.all_gather(logits.T.reshape(tile), axes)]
    all_to_all x2 -> x0, blocking collectives: 167 us -> none  [the longest x1 85.5 us: on_device(): lax.all_to_all(sent, 'expert', split_axis=0, concat_axis=0, tiled=True)]
    all_to_all x1, waiting for transfers between devices: 0.01 us -> 70.4 us  [on_device(): lax.all_to_all(out_rows.reshape(received.shape), 'expert', split_axis=0,...]
    all_to_all x1, waiting for transfers between devices: 0.01 us -> 60.8 us  [on_device(): lax.all_to_all(sent_grad, 'expert', split_axis=0, concat_axis=0, tiled=True)]
    all_to_all x0 -> x2, waiting for transfers between devices: none -> 54.6 us  [the longest x1 54.6 us: on_device(): lax.all_to_all(back_grad, 'expert', split_axis=0, concat_axis=0, tiled=True)]
    reduce_sum x31 -> x1, other arithmetic: 41.6 us -> 0.73 us  [on_device(): gate = jnp.sum(probs * selected, axis=0)]
    pallas_call x0 -> x2, Pallas kernels: none -> 13.8 us  [in_vmem(): pl.pallas_call(kernel, out_shape=outs, in_specs=[pl.BlockSpec(memory_spac...]
  transfers between devices with their start and end apart: 4 -> 6, of which waited for: 0 -> 3; matrix products, arithmetic and copies ran while one was open for 10% -> 19% of each run, Pallas kernels for 0% -> 2%
where the time goes in v1:
time: 683 us; the launch traced here: 674 us
  blocking collectives  258 us (38%)
  waiting for transfers between devices  186 us (27%)
  matrix products  120 us (18%)
  other arithmetic  42.3 us (6%)
  local copies, waits for them, and re-layouts  20.7 us (3%)
  starting transfers between devices  19.6 us (3%)
  between operations  14.6 us (2%)
  Pallas kernels  13.8 us (2%)
    all_gather x1, blocking collectives, on_device(): all_logits = lax.all_gather(logits.T.reshape(tile), axes)  145 us
    all_gather x1, blocking collectives, on_device(): all_grads = lax.all_gather(probs_grad.reshape(tile), axes)  74.8 us
    all_to_all x1, waiting for transfers between devices, on_device(): lax.all_to_all(out_rows.reshape(received.shape), 'expert', split_axis=0,...  70.4 us
    all_to_all x1, waiting for transfers between devices, on_device(): lax.all_to_all(sent_grad, 'expert', split_axis=0, concat_axis=0, tiled=True)  60.8 us
    all_to_all x1, waiting for transfers between devices, on_device(): lax.all_to_all(back_grad, 'expert', split_axis=0, concat_axis=0, tiled=True)  54.6 us
    dot_general x2, matrix products, contract_last(): lax.dot_general(left, right, (((1,), (1,)), ((), ())), preferred_element_...  38.9 us
    psum x1, blocking collectives, on_device(): lax.psum((gain_local, router_local), ('dp', 'expert'))  38.3 us
    dot_general x2, matrix products, contract_first(): lax.dot_general(left, right, (((0,), (0,)), ((), ())), preferred_element_...  33.9 us
  transfers between devices with their start and end apart: 6, of which 3 were waited for; matrix products, arithmetic and copies ran while one was open for 19% of the time, Pallas kernels for 2%

profile of v1, /device:TPU:0, one launch (start us, length us, event | category | flops | bytes accessed | tf_op | source)
XLA Modules:
  0.0 674.4 jit_solution(4521058604910287340)
XLA Ops:
  13.7 8.8 %scatter_custom_fusion = bf16[1536,1152]{1,0:T(8,128)(2,1)} fusion(s32[1024]{0:T(1024)S(1)} %bitcast.97, bf16[]{:T(256)} %constant.19.clone.1, bf16[1024,1152]{1,0:T(8,128)(2,1)} %param.9, f32[1152]{0:T(1024)} %param.10, f32[1024]{0:T(1024)S(1)} %add_rsqrt_fusion), kind=kCustom, calls=%fused_computation.46 | custom fusion | flops 4718592 | bytes 5906946 | tf_op jit(solution)/shard_map/scatter | solution.py:166
  22.5 6.4 all-to-all-start
  30.4 144.5 %all_gather.6.logits_ref = f32[32,4,8,128]{3,2,1,0:T(8,128)} all-gather(f32[1,4,8,128]{3,2,1,0:T(8,128)S(1)} %copy.23), channel_id=1, replica_groups=mesh['dp'=8,'expert'=4] {'dp','expert'}, dimensions={0}, use_global_device_ids=true | all-gather | bytes 540672 | tf_op jit(solution)/shard_map/all_gather | solution.py:144
  174.9 6.8 %shard_map.118 = (f32[32,4,8,128]{3,2,1,0:T(8,128)}, f32[8,32,8,128]{3,2,1,0:T(8,128)}, f32[8,4,8,128]{3,2,1,0:T(8,128)}) custom-call(f32[32,4,8,128]{3,2,1,0:T(8,128)} %all_gather.6.logits_ref), custom_call_target="tpu_custom_call" | custom-call | tf_op jit(solution)/shard_map/pallas_call | solution.py:107
  182.5 9.4 %scatter_custom_fusion.1 = f32[1536,1152]{1,0:T(8,128)} fusion(s32[1024]{0:T(1024)S(1)} %bitcast.98, bf16[1024,1152]{1,0:T(8,128)(2,1)} %param.15, f32[]{:T(128)} %constant.26.clone.1, f32[1024]{0:T(1024)S(1)} %bitcast.92), kind=kCustom, calls=%fused_computation.41 | custom fusion | flops 2359296 | bytes 9441284 | tf_op jit(solution)/shard_map/scatter | solution.py:194
  191.9 5.2 convert_element_type.61
  201.1 19.6 %multiply_convert_fusion = (bf16[1536,3072]{1,0:T(8,128)(2,1)}, f32[1536,3072]{1,0:T(8,128)}) fusion(bf16[1536,1152]{1,0:T(8,128)(2,1)} %bitcast.8, bf16[1,1152,3072]{2,1,0:T(8,128)(2,1)} %param.12), kind=kOutput, calls=%fused_computation.11 | convolution fusion | flops 10895228928 | bytes 38928384 | tf_op jit(solution)/shard_map/dot_general | solution.py:172
  220.7 54.6 %all-to-all-done.2 = bf16[4,384,1152]{2,1,0:T(8,128)(2,1)S(1)} async-done(((bf16[4,384,1152]{2,1,0:T(8,128)(2,1)}), bf16[4,384,1152]{2,1,0:T(8,128)(2,1)S(1)}, u32[]{:S(2)}, u32[]{:S(2)}) %all-to-all-start.2) | async-done | bytes 3538976 | tf_op jit(solution)/shard_map/all_to_all | solution.py:197
  275.3 20.5 %fusion.5 = bf16[1536,3072]{1,0:T(8,128)(2,1)S(1)} fusion(f32[1536,3072]{1,0:T(8,128)} %get-tuple-element.20, bf16[1536,1152]{1,0:T(8,128)(2,1)S(1)} %bitcast.81, bf16[1,3072,1152]{2,1,0:T(8,128)(2,1)} %param.13), kind=kOutput, calls=%fused_computation.10 | convolution fusion | flops 10918821888 | bytes 38928384 | tf_op jit(solution)/shard_map/dot_general | solution.py:118
  299.4 16.1 %convolution_bitcast_fusion = f32[1,1152,3072]{2,1,0:T(8,128)} fusion(bf16[1536,1152]{1,0:T(8,128)(2,1)} %bitcast.8, bf16[1536,3072]{1,0:T(8,128)(2,1)S(1)} %fusion.5), kind=kOutput, calls=%fused_computation.13 | convolution fusion | flops 10871635968 | bytes 27131904 | tf_op jit(solution)/shard_map/dot_general | solution.py:124
  315.8 17.9 %convolution_bitcast_fusion.1 = f32[1,3072,1152]{2,1,0:T(8,128)} fusion(bf16[1536,3072]{1,0:T(8,128)(2,1)} %get-tuple-element.19, bf16[1536,1152]{1,0:T(8,128)(2,1)S(1)} %bitcast.82), kind=kOutput, calls=%fused_computation.14 | convolution fusion | flops 10871635968 | bytes 27131904 | tf_op jit(solution)/shard_map/dot_general | solution.py:124
  333.7 18.4 %convolution_convert_fusion = bf16[1536,1152]{1,0:T(8,128)(2,1)} fusion(bf16[1536,3072]{1,0:T(8,128)(2,1)} %copy-done.15, bf16[1,1152,3072]{2,1,0:T(8,128)(2,1)} %param.12), kind=kOutput, calls=%fused_computation.15 | convolution fusion | flops 10873405440 | bytes 20054016 | tf_op jit(solution)/shard_map/dot_general | solution.py:118
  355.8 18.1 %convolution_convert_fusion.1 = bf16[1536,1152]{1,0:T(8,128)(2,1)} fusion(bf16[1536,3072]{1,0:T(8,128)(2,1)} %get-tuple-element.19, bf16[1,3072,1152]{2,1,0:T(8,128)(2,1)} %param.13), kind=kOutput, calls=%fused_computation.16 | convolution fusion | flops 10873405440 | bytes 20054016 | tf_op jit(solution)/shard_map/dot_general | solution.py:174
  373.9 60.8 %all-to-all-done.3 = bf16[4,384,1152]{2,1,0:T(8,128)(2,1)S(1)} async-done(((bf16[4,384,1152]{2,1,0:T(8,128)(2,1)}), bf16[4,384,1152]{2,1,0:T(8,128)(2,1)S(1)}, u32[]{:S(2)}, u32[]{:S(2)}) %all-to-all-start.3) | async-done | bytes 3538976 | tf_op jit(solution)/shard_map/all_to_all | solution.py:204
  434.8 5.2 all-to-all-start.1
  442.5 5.7 gather_fusion.1
  448.1 70.4 %all-to-all-done.1 = bf16[4,384,1152]{2,1,0:T(8,128)(2,1)} async-done(((bf16[4,384,1152]{2,1,0:T(8,128)(2,1)}), bf16[4,384,1152]{2,1,0:T(8,128)(2,1)}, u32[]{:S(2)}, u32[]{:S(2)}) %all-to-all-start.1) | async-done | bytes 3538976 | tf_op jit(solution)/shard_map/all_to_all | solution.py:175
  518.5 9.2 %gather_fusion = bf16[1024,1152]{1,0:T(8,128)(2,1)} fusion(bf16[1536,1152]{1,0:T(8,128)(2,1)} %bitcast.12, s32[1024]{0:T(1024)} %broadcast_clamp_fusion), kind=kCustom, calls=%fused_computation.clone | custom fusion | bytes 4722688 | tf_op jit(solution)/shard_map/jit(_take)/gather | solution.py:185
  527.8 4.7 fusion.23
  532.5 74.8 %all_gather.7.grads_ref = f32[32,4,8,128]{3,2,1,0:T(8,128)} all-gather(f32[1,4,8,128]{3,2,1,0:T(8,128)S(1)} %fusion.30), channel_id=1, replica_groups=mesh['dp'=8,'expert'=4] {'dp','expert'}, dimensions={0}, use_global_device_ids=true | all-gather | bytes 540672 | tf_op jit(solution)/shard_map/all_gather | solution.py:212
  607.3 7.0 %shard_map.119 = f32[32,4,8,128]{3,2,1,0:T(8,128)} custom-call(f32[32,4,8,128]{3,2,1,0:T(8,128)} %get-tuple-element.10.probs_ref, f32[8,32,8,128]{3,2,1,0:T(8,128)} %get-tuple-element.11.rows_ref, f32[8,4,8,128]{3,2,1,0:T(8,128)} %get-tuple-element.12.scales_ref, f32[32,4,8,128]{3,2,1,0:T(8,128)} %all_gather.7.grads_ref), custom_call_target="tpu_custom_call" | custom-call | tf_op jit(solution)/shard_map/pallas_call | solution.py:107
  616.3 7.2 %fusion.19 = (f32[1152]{0:T(1024)S(1)}, f32[1024]{0:T(1024)S(1)}, f32[1024,1152]{1,0:T(8,128)}) fusion(bf16[1024,1152]{1,0:T(8,128)(2,1)S(1)} %copy-done.2, f32[1024]{0:T(1024)S(1)} %copy-done.9, f32[1152]{0:T(1024)S(1)} %copy-done.11, bf16[1152,4]{0,1:T(4,128)(2,1)S(1)} %copy-done, f32[1,4,8,128]{3,2,1,0:T(8,128)S(1)} %dynamic-slice_bitcast_fusion, ...), kind=kOutput, calls=%fused_computation.38 | convolution fusion | flops 68421504 | bytes 9497600 | tf_op jit(solution)/shard_map/dot_general | solution.py:227
  623.5 38.3 %all-reduce = (f32[1152]{0:T(1024)}, f32[1152,4]{0,1:T(4,128)}) all-reduce(f32[1152]{0:T(1024)S(1)} %get-tuple-element.13, f32[1152,4]{0,1:T(4,128)S(1)} %fusion.31), channel_id=1, replica_groups=mesh['dp'=8,'expert'=4] {'dp','expert'}, use_global_device_ids=true, to_apply=%region_10.12 | all-reduce | flops 5760 | bytes 46080 | tf_op jit(solution)/shard_map/psum | solution.py:234
  661.8 5.3 convert_add_fusion
  (59 shorter events, 24.9 us)
Async XLA Ops:
  7.2 21.8 %copy-start = (bf16[1152,4]{0,1:T(4,128)(2,1)S(1)}, bf16[1152,4]{0,1:T(4,128)(2,1)}, u32[]{:S(2)}) copy-start(bf16[1152,4]{0,1:T(4,128)(2,1)} %param.11) | copy-start | bytes 27652
  9.4 19.6 %copy-start.8 = (f32[1024]{0:T(1024)}, f32[1024]{0:T(1024)S(1)}, u32[]{:S(2)}) copy-start(f32[1024]{0:T(1024)S(1)} %add_rsqrt_fusion) | copy-start | bytes 12292
  12.4 0.6 copy-start.5
  22.5 6.5 copy-start.1
  22.5 6.5 copy-start.10
  22.5 159.3 %copy-start.3 = (s32[1024,1]{0,1:T(1,128)S(1)}, s32[1024,1]{0,1:T(1,128)}, u32[]{:S(2)}) copy-start(s32[1024,1]{0,1:T(1,128)} %param.14) | copy-start | bytes 12292
  22.5 174.6 %all-to-all-start = ((bf16[4,384,1152]{2,1,0:T(8,128)(2,1)}), bf16[4,384,1152]{2,1,0:T(8,128)(2,1)}, u32[]{:S(2)}, u32[]{:S(2)}) async-start(bf16[4,384,1152]{2,1,0:T(8,128)(2,1)} %bitcast.80), calls=%async_computation | async-start | bytes 7077888 | tf_op jit(solution)/shard_map/all_to_all | solution.py:170
  29.8 0.6 copy-start.12
  182.5 9.4 %copy-start.6 = (f32[8,128]{1,0:T(8,128)}, f32[8,128]{1,0:T(8,128)S(1)}, u32[]{:S(2)}) copy-start(f32[8,128]{1,0:T(8,128)S(1)} %select_reduce_fusion) | copy-start | bytes 12292
  197.1 78.2 %all-to-all-start.2 = ((bf16[4,384,1152]{2,1,0:T(8,128)(2,1)}), bf16[4,384,1152]{2,1,0:T(8,128)(2,1)S(1)}, u32[]{:S(2)}, u32[]{:S(2)}) async-start(bf16[4,384,1152]{2,1,0:T(8,128)(2,1)} %bitcast.13), calls=%async_computation.2 | async-start | bytes 7077888 | tf_op jit(solution)/shard_map/all_to_all | solution.py:197
  200.9 466.3 %reduce-scatter.3.cloned.1.call-start = ((), (), s32[]{:S(2)}) async-start(), calls=%async_computation.6 | async-start | bytes 15925248 | tf_op jit(solution)/shard_map/reduce_scatter | solution.py:208
  295.8 3.6 copy-start.15
  315.5 351.6 %reduce-scatter.5.cloned.1.call-start = ((), (), s32[]{:S(2)}) async-start(), calls=%async_computation.7 | async-start | bytes 15925248 | tf_op jit(solution)/shard_map/reduce_scatter | solution.py:209
  352.0 82.7 %all-to-all-start.3 = ((bf16[4,384,1152]{2,1,0:T(8,128)(2,1)}), bf16[4,384,1152]{2,1,0:T(8,128)(2,1)S(1)}, u32[]{:S(2)}, u32[]{:S(2)}) async-start(bf16[4,384,1152]{2,1,0:T(8,128)(2,1)} %bitcast.84), calls=%async_computation.3 | async-start | bytes 7077888 | tf_op jit(solution)/shard_map/all_to_all | solution.py:204
  373.9 66.0 %copy-start.4 = (s32[1024,1]{0,1:T(1,128)S(1)}, s32[1024,1]{0,1:T(1,128)}, u32[]{:S(2)}) copy-start(s32[1024,1]{0,1:T(1,128)} %param.14) | copy-start | bytes 12292
  434.8 83.7 %all-to-all-start.1 = ((bf16[4,384,1152]{2,1,0:T(8,128)(2,1)}), bf16[4,384,1152]{2,1,0:T(8,128)(2,1)}, u32[]{:S(2)}, u32[]{:S(2)}) async-start(bf16[4,384,1152]{2,1,0:T(8,128)(2,1)} %bitcast.83), calls=%async_computation.1 | async-start | bytes 7077888 | tf_op jit(solution)/shard_map/all_to_all | solution.py:175
  518.5 9.3 %copy-start.2 = (bf16[1024,1152]{1,0:T(8,128)(2,1)S(1)}, bf16[1024,1152]{1,0:T(8,128)(2,1)}, u32[]{:S(2)}) copy-start(bf16[1024,1152]{1,0:T(8,128)(2,1)} %param.9) | copy-start | bytes 7077892
  518.5 9.3 %copy-start.7 = (f32[8,128]{1,0:T(8,128)S(1)}, f32[8,128]{1,0:T(8,128)}, u32[]{:S(2)}) copy-start(f32[8,128]{1,0:T(8,128)} %copy-done.6) | copy-start | bytes 12292
  518.5 9.3 %copy-start.14 = (pred[1024]{0:T(1024)(128)(4,1)S(1)}, pred[1024]{0:T(1024)(128)(4,1)}, u32[]{:S(2)}) copy-start(pred[1024]{0:T(1024)(128)(4,1)} %compare_and_fusion) | copy-start | bytes 3076
  527.8 87.2 %copy-start.9 = (f32[1024]{0:T(1024)S(1)}, f32[1024]{0:T(1024)}, u32[]{:S(2)}) copy-start(f32[1024]{0:T(1024)} %copy-done.8) | copy-start | bytes 12292
  527.8 87.2 %copy-start.11 = (f32[1152]{0:T(1024)S(1)}, f32[1152]{0:T(1024)}, u32[]{:S(2)}) copy-start(f32[1152]{0:T(1024)} %param.10) | copy-start | bytes 13828
  527.8 87.2 %copy-start.13 = (f32[1024,4]{0,1:T(4,128)S(1)}, f32[1024,4]{0,1:T(4,128)}, u32[]{:S(2)}) copy-start(f32[1024,4]{0,1:T(4,128)} %copy-done.12) | copy-start | bytes 49156
Sparse Core Ops, SparseCore 0:
  315.6 99.6 reduce-scatter.2
  419.4 100.7 reduce-scatter.4
